TPU v7x, 128 devices: a whole 4x4x4 slice. The times are simulated.
128 devices in a mesh: row: 8 (over x, core), col: 16 (over y, z).
Axes of the slice: x: 4, y: 4, z: 4, core: 2. Of those that a mesh axis runs over, the one named last changes fastest.
Arguments:
- left_tiles: bfloat16 [8192, 4096], P('row', 'col'), may hold values from -6 to 6
- right_tiles: bfloat16 [4096, 16384], P('row', 'col'), may hold values from -0.09375 to 0.09375
- left_mask: int32 [64, 32], P('row', 'col'), may hold values from 0 to 1, as said below
- right_mask: int32 [32, 128], P('row', 'col'), may hold values from 0 to 1, as said below
- cycle_weight: bfloat16 [16384, 1024], P('col', 'row'), may hold values from -0.046875 to 0.046875
Outputs:
- cycle_out: float32 [64, 128, 1024], P('row', 'col')
Inputs may be any that keep to these rules, and one draw needn't show every extreme that they name: `left_mask`: each tile row i keeps each of its tiles with chance one, two or three thirds, the level drawn per row. `right_mask`: each tile column a keeps each of its tiles with chance one, two or three thirds, the level drawn per column.
All inputs are finite; a program needn't handle non-finite values.
Results may differ from a plain program's by a relative error of at most 0.0029.
Values may be sent and summed in bfloat16 or wider, within the bound.
A program may use at most 64 MiB of HBM per device.

v0:
```python
import jax
import jax.numpy as jnp
from jax import lax
from jax.sharding import PartitionSpec as P

JOCC = 128
VIRT_B = 128


def apply_mask(tiles, mask):
    rows, cols = tiles.shape
    mrows, mcols = mask.shape
    shaped = tiles.reshape(mrows, rows // mrows, mcols, cols // mcols)
    return (shaped * mask[:, None, :, None].astype(tiles.dtype)).reshape(rows, cols)


def body(left_tiles, right_tiles, left_mask, right_mask, cycle_weight):
    masked_left = apply_mask(left_tiles, left_mask)
    masked_right = apply_mask(right_tiles, right_mask)
    gathered = lax.all_gather(masked_left, "col", axis=1, tiled=True)
    totals = jnp.dot(
        gathered,
        lax.all_gather(masked_right, "row", axis=0, tiled=True),
        preferred_element_type=jnp.float32,
    )
    occ_local = left_mask.shape[0]
    vir_local = right_mask.shape[1]
    pair_block = totals.astype(jnp.bfloat16).reshape(occ_local, JOCC, vir_local, VIRT_B)
    relaid = lax.all_to_all(pair_block, "col", split_axis=1, concat_axis=2, tiled=True)
    piece = lax.all_gather(cycle_weight, "row", axis=1, tiled=True)
    operand = piece.reshape(piece.shape[0] // VIRT_B, VIRT_B, piece.shape[1])
    cycle_terms = jnp.einsum("ijab,jbk->iak", relaid, operand, preferred_element_type=jnp.float32)
    return lax.psum_scatter(cycle_terms, "col", scatter_dimension=1, tiled=True)


def solution(mesh):
    placed = (P("row", "col"), P("row", "col"), P("row", "col"), P("row", "col"), P("col", "row"))
    return jax.shard_map(
        body, mesh=mesh, in_specs=placed, out_specs=P("row", "col", None), check_vma=False
    )
```

profile of v0, /device:TPU:1, one launch (start us, length us, event | category | flops | bytes accessed | tf_op | source)
XLA Modules:
  0.0 280.1 jit_solution(11570222039503494329)
XLA Ops:
  6.5 0.0 all-gather.6.cloned.1.call-start
  6.5 0.7 convert_element_type.12
  7.2 0.2 mul.25
  7.4 0.0 copy-start.1
  7.4 0.0 copy-start
  7.5 2.4 bitcast_multiply_fusion
  9.9 0.0 all-gather.6.cloned.1.call-update
  9.9 0.0 all-gather.4.cloned.1.call-start
  9.9 0.0 copy-done.1
  9.9 0.1 copy.8
  10.0 0.3 mul.22
  10.4 0.0 copy-done
  10.4 0.9 bitcast_multiply_fusion.1
  11.3 0.0 all-gather.4.cloned.1.call-update
  11.3 0.0 all-gather.8.cloned.1.call-start
  11.4 0.7 all-gather.8.cloned.1.call-update
  12.0 51.3 %all-gather.6.cloned.1.call-done = bf16[4096,1024]{1,0:T(8,128)(2,1)} async-done(((bf16[512,1024]{1,0:T(8,128)(2,1)}), bf16[4096,1024]{1,0:T(8,128)(2,1)}) %all-gather.6.cloned.1.call-update) | async-done | bytes 8388624 | tf_op jit(solution)/shard_map/all_gather | solution.py:23
  63.3 79.6 %all-gather.4.cloned.1.call-done = bf16[1024,4096]{1,0:T(8,128)(2,1)} async-done(((bf16[1024,256]{1,0:T(8,128)(2,1)}), bf16[1024,4096]{1,0:T(8,128)(2,1)}) %all-gather.4.cloned.1.call-update) | async-done | bytes 8388624 | tf_op jit(solution)/shard_map/all_gather | solution.py:20
  142.9 13.7 %convert_bitcast_fusion = bf16[128,8,8,128]{3,1,2,0:T(8,128)(2,1)S(1)} fusion(bf16[1024,4096]{1,0:T(8,128)(2,1)} %all-gather.4.cloned.1.call-done, bf16[4096,1024]{1,0:T(8,128)(2,1)} %all-gather.6.cloned.1.call-done), kind=kOutput, calls=%fused_computation.3 | convolution fusion | flops 8590983168 | bytes 18874368 | tf_op jit(solution)/shard_map/dot_general | solution.py:21
  156.6 0.6 copy.14
  157.2 1.9 copy.9
  159.1 4.7 %all-to-all-start = ((bf16[8,128,8,128]{3,2,0,1:T(8,128)(2,1)}), bf16[8,128,8,128]{3,2,0,1:T(8,128)(2,1)S(1)}, u32[]{:S(2)}, u32[]{:S(2)}) async-start(bf16[8,128,8,128]{3,2,0,1:T(8,128)(2,1)} %copy.9), calls=%async_computation | async-start | bytes 4194304 | tf_op jit(solution)/shard_map/all_to_all | solution.py:29
  163.8 0.0 reduce-scatter.2.cloned.1.call-start
  163.9 8.5 %all-gather.8.cloned.1.call-done = bf16[1024,1024]{1,0:T(8,128)(2,1)} async-done(((bf16[1024,128]{1,0:T(8,128)(2,1)}), bf16[1024,1024]{1,0:T(8,128)(2,1)}) %all-gather.8.cloned.1.call-update) | async-done | bytes 2097168 | tf_op jit(solution)/shard_map/all_gather | solution.py:30
  172.4 17.1 %all-to-all-done = bf16[8,128,8,128]{3,2,0,1:T(8,128)(2,1)S(1)} async-done(((bf16[8,128,8,128]{3,2,0,1:T(8,128)(2,1)}), bf16[8,128,8,128]{3,2,0,1:T(8,128)(2,1)S(1)}, u32[]{:S(2)}, u32[]{:S(2)}) %all-to-all-start) | async-done | bytes 2097184 | tf_op jit(solution)/shard_map/all_to_all | solution.py:29
  189.4 5.4 %convolution_bitcast_fusion = f32[8,128,1024]{2,1,0:T(8,128)} fusion(bf16[8,128,1024,1]{2,1,0,3:T(8,128)(2,1)} %bitcast.31, bf16[8,16,8,8,128]{4,3,0,2,1:T(8,128)(2,1)S(1)} %bitcast.30), kind=kOutput, calls=%fused_computation | convolution fusion | flops 2147483648 | bytes 8388608 | tf_op jit(solution)/shard_map/ijab,jbk->iak/dot_general | solution.py:32
  194.9 0.0 reduce-scatter.2.cloned.1.call-update
  194.9 78.7 %reduce-scatter.2.cloned.1.call-done = f32[8,8,1024]{2,1,0:T(8,128)} async-done(((f32[8,128,1024]{2,1,0:T(8,128)}), f32[8,8,1024]{2,1,0:T(8,128)}) %reduce-scatter.2.cloned.1.call-update) | async-done | bytes 262160 | tf_op jit(solution)/shard_map/reduce_scatter | solution.py:33
  (1 shorter events, 0.0 us)
Async XLA Ops:
  6.5 56.8 %all-gather.6.cloned.1.call-start = ((), (), s32[]{:S(2)}) async-start(), calls=%async_computation.3 | async-start | bytes 9437184 | tf_op jit(solution)/shard_map/all_gather | solution.py:23
  7.4 2.5 copy-start.1
  7.4 2.9 %copy-start = (bf16[1024,256]{1,0:T(8,128)(2,1)S(1)}, bf16[1024,256]{1,0:T(8,128)(2,1)}, u32[]{:S(2)}) copy-start(bf16[1024,256]{1,0:T(8,128)(2,1)} %param.5) | copy-start | bytes 1572868
  9.9 133.0 %all-gather.4.cloned.1.call-start = ((), (), s32[]{:S(2)}) async-start(), calls=%async_computation.2 | async-start | bytes 8912896 | tf_op jit(solution)/shard_map/all_gather | solution.py:20
  11.3 161.1 %all-gather.8.cloned.1.call-start = ((), (), s32[]{:S(2)}) async-start(), calls=%async_computation.4 | async-start | bytes 2359296 | tf_op jit(solution)/shard_map/all_gather | solution.py:30
  159.1 30.3 %all-to-all-start = ((bf16[8,128,8,128]{3,2,0,1:T(8,128)(2,1)}), bf16[8,128,8,128]{3,2,0,1:T(8,128)(2,1)S(1)}, u32[]{:S(2)}, u32[]{:S(2)}) async-start(bf16[8,128,8,128]{3,2,0,1:T(8,128)(2,1)} %copy.9), calls=%async_computation | async-start | bytes 4194304 | tf_op jit(solution)/shard_map/all_to_all | solution.py:29
  163.8 109.8 %reduce-scatter.2.cloned.1.call-start = ((), (), s32[]{:S(2)}) async-start(), calls=%async_computation.5 | async-start | bytes 4456448 | tf_op jit(solution)/shard_map/reduce_scatter | solution.py:33
Sparse Core Ops, SparseCore 0:
  10.0 53.3 all-gather.5
  65.5 77.4 all-gather.3
  144.6 27.7 all-gather.7
  195.0 78.5 reduce-scatter.1
where the time goes:
time: 281 us; the launch traced here: 280 us
  waiting for transfers between devices  236 us (84%)
  matrix products  19.1 us (7%)
  between operations  13.2 us (5%)
  starting transfers between devices  4.79 us (2%)
  other arithmetic  3.97 us (1%)
  local copies, waits for them, and re-layouts  3.2 us (1%)
    all_gather x1, waiting for transfers between devices, body(): gathered = lax.all_gather(masked_left, 'col', axis=1, tiled=True)  79.6 us
    reduce_scatter x1, waiting for transfers between devices, body(): return lax.psum_scatter(cycle_terms, 'col', scatter_dimension=1, tiled=True)  78.7 us
    all_gather x1, waiting for transfers between devices, body(): lax.all_gather(masked_right, 'row', axis=0, tiled=True)  51.3 us
    all_to_all x1, waiting for transfers between devices, body(): lax.all_to_all(pair_block, 'col', split_axis=1, concat_axis=2, tiled=True)  17.1 us
    dot_general x1, matrix products, body(): jnp.dot(gathered, lax.all_gather(masked_right, 'row', axis=0, tiled=True)...  13.7 us
    all_gather x1, waiting for transfers between devices, body(): piece = lax.all_gather(cycle_weight, 'row', axis=1, tiled=True)  8.5 us
  transfers between devices with their start and end apart: 5, of which 5 were waited for; matrix products, arithmetic and copies ran while one was open for 6% of the time, Pallas kernels for 0%

commit v1 on v0

v1 whole, which is shorter than its diff:
```python
import jax
import jax.numpy as jnp
from jax import lax
from jax.experimental import pallas as pl
from jax.experimental.pallas import tpu as pltpu
from jax.sharding import PartitionSpec as P

MESH = pl.DeviceIdType.MESH
F32 = jnp.float32
BF16 = jnp.bfloat16

GROUPS = (0, 2, -1, 1)
ITEMS = (("L", 0), ("L", 1), ("W", 0), ("W", 1), ("L", 2), ("L", 3))
LAG = 3
STAGES = 7


def norm(d):
    return (d + 1) % 4 - 1


def kernel(l_ref, r_ref, w_ref, lm_ref, rm_ref, out_ref,
           L, R, W, lf, lp, acc, lhs, part, sib, far,
           g_send, g_recv, a_send, a_recv, r_send, r_recv, s_send, s_recv, o_send, o_recv):
    row, col = lax.axis_index("row"), lax.axis_index("col")
    x, core = row // 2, row % 2
    y, z = col // 4, col % 4
    sent = []

    def row_at(dx, e):
        other = core if e == 0 else 1 - core
        return ((x + dx + 4) % 4) * 2 + other

    def col_at(dy, dz):
        return ((y + dy + 4) % 4) * 4 + (z + dz + 4) % 4

    def put(src, dst, send, recv, device):
        copy = pltpu.make_async_remote_copy(
            src_ref=src, dst_ref=dst, send_sem=send, recv_sem=recv,
            device_id=device, device_id_type=MESH)
        copy.start()
        sent.append(copy)

    def arrived(dst, send, recv):
        pltpu.make_async_remote_copy(
            src_ref=dst, dst_ref=dst, send_sem=send, recv_sem=recv,
            device_id=(row_at(0, 1), col), device_id_type=MESH).wait_recv()

    barrier = pltpu.get_barrier_semaphore()
    peers = [(row, col_at(1, 0)), (row, col_at(-1, 0)), (row, col_at(0, 1)), (row, col_at(0, -1))]
    peers += [(row_at(dx, e), col) for dx in GROUPS for e in (0, 1) if (dx, e) != (0, 0)]
    for peer in peers:
        pl.semaphore_signal(barrier, inc=1, device_id=peer, device_id_type=MESH)

    for i in range(8):
        for t in range(2):
            keep = lm_ref[i, t].astype(F32)
            lf[t, i * 128:(i + 1) * 128, :] = l_ref[i * 128:(i + 1) * 128, t * 128:(t + 1) * 128].astype(F32) * keep
    for r in range(8):
        for t in range(2):
            for q in range(0, 16, 2):
                pair = [lf[t, pl.ds(8 * (q + s) + r, 8, stride=128), :] for s in (0, 1)]
                lp[r, q * 8:q * 8 + 16, t * 128:(t + 1) * 128] = jnp.concatenate(pair, axis=0).astype(BF16)
    for t in range(4):
        here = pl.ds(pl.multiple_of(row * 512 + t * 128, 128), 128)
        for a in range(8):
            keep = rm_ref[t, a].astype(F32)
            R[here, a * 128:(a + 1) * 128] = (r_ref[t * 128:(t + 1) * 128, a * 128:(a + 1) * 128].astype(F32) * keep).astype(BF16)
    own_l = pl.ds(pl.multiple_of(col * 256, 256), 256)
    own_w = pl.ds(pl.multiple_of(col * 128, 128), 128)
    row_w = pl.ds(pl.multiple_of(row * 128, 128), 128)
    L[0, :, own_l] = lp[row]
    W[own_w, row_w] = w_ref[row_w, :]

    pl.semaphore_wait(barrier, len(peers))

    def exchange_l(g, e):
        dx = GROUPS[g]
        slot = 2 * GROUPS.index(norm(-dx)) + e
        to = row_at(dx, e)
        put(lp.at[to], L.at[slot, :, own_l], a_send.at[0, 2 * g + e], a_recv.at[0, slot], (to, col))

    def exchange_w(g, e):
        dx = GROUPS[g]
        slot = 2 * GROUPS.index(norm(-dx)) + e
        to = row_at(dx, e)
        put(w_ref.at[pl.ds(pl.multiple_of(to * 128, 128), 128), :], W.at[own_w, row_w],
            a_send.at[1, 2 * g + e], a_recv.at[1, slot], (to, col))

    def exchanged_l(slot):
        arrived(L.at[slot, :, own_l], a_send.at[0, slot], a_recv.at[0, slot])

    def exchanged_w(slot):
        g, e = slot // 2, slot % 2
        lanes = pl.ds(pl.multiple_of(row_at(GROUPS[g], e) * 128, 128), 128)
        arrived(W.at[own_w, lanes], a_send.at[1, slot], a_recv.at[1, slot])

    def r_piece(dx, e, p):
        return R.at[pl.ds(pl.multiple_of(row_at(dx, e) * 512 + p * 128, 128), 128), :]

    r_count = [0]

    def r_put(dx, p, to):
        view = r_piece(dx, 0, p)
        if to is None:
            recv, device = s_recv.at[GROUPS.index(dx), p], (row_at(0, 1), col)
        else:
            recv, device = r_recv.at[GROUPS.index(norm(dx - to)), p], (row_at(to, 0), col)
        put(view, view, r_send.at[r_count[0]], recv, device)
        r_count[0] += 1

    def r_arrived(dx, p):
        arrived(r_piece(dx, 0, p), r_send.at[0], r_recv.at[GROUPS.index(dx), p])

    def r_stage0(p):
        r_put(0, p, 1)
        r_put(0, p, -1)
        r_put(0, p, None)

    def r_stage1(p):
        r_arrived(-1, p)
        if p < 2:
            r_put(-1, p, 1)
        r_put(-1, p, None)
        r_arrived(1, p)
        if p >= 2:
            r_put(1, p, -1)
        r_put(1, p, None)

    def r_stage2(p):
        r_arrived(2, p)
        r_put(2, p, None)

    def r_stage3():
        for dx in GROUPS:
            for p in range(4):
                arrived(r_piece(dx, 1, p), s_send, s_recv.at[GROUPS.index(dx), p])

    def block(n, h, at):
        kind, g = ITEMS[n]
        if kind == "L":
            return L.at[2 * g + h, :, pl.ds(pl.multiple_of(at * 256, 256), 256)]
        return W.at[pl.ds(pl.multiple_of(at * 128 + (2 * g + h) * 32, 32), 32), :]

    def along(h, p, q):
        return col_at(p, q) if h == 0 else col_at(q, p)

    def sem_of(p, q):
        return 4 * (p % 4) + q % 4

    counts = {}

    def g_put(n, h, p, q, ep, eq):
        view = block(n, h, along(h, p, q))
        k = counts.get((n, h), 0)
        counts[n, h] = k + 1
        put(view, view, g_send.at[n, h, k], g_recv.at[n, h, sem_of(p - ep, q - eq)], (row, along(h, ep, eq)))

    def g_arrived(n, h, p, q):
        arrived(block(n, h, along(h, p, q)), g_send.at[n, h, 0], g_recv.at[n, h, sem_of(p, q)])

    def stage(n, k):
        if k == 0:
            kind, g = ITEMS[n]
            if kind == "W" and g == 0:
                for slot in range(1, 8):
                    exchanged_w(slot)
        for h in (0, 1):
            if k == 0:
                if kind == "L" and 2 * g + h > 0:
                    exchanged_l(2 * g + h)
                for e in (1, -1):
                    g_put(n, h, 0, 0, e, 0)
                    g_put(n, h, 0, 0, 0, e)
            elif k == 1:
                way = 1 if n % 2 == 0 else -1
                for d in (-1, 1):
                    g_arrived(n, h, d, 0)
                    if d == -way:
                        g_put(n, h, d, 0, way, 0)
                    for e in (1, -1):
                        g_put(n, h, d, 0, 0, e)
            elif k == 2:
                g_arrived(n, h, 0, -1)
                g_put(n, h, 0, -1, 0, 1)
                g_arrived(n, h, 0, 1)
            elif k == 3:
                g_arrived(n, h, 2, 0)
                for e in (1, -1):
                    g_put(n, h, 2, 0, 0, e)
            elif k == 4:
                for d in (-1, 1):
                    g_arrived(n, h, d, 1)
                    g_put(n, h, d, 1, 0, -1)
                    g_arrived(n, h, d, -1)
            elif k == 5:
                g_arrived(n, h, 2, -1)
                g_put(n, h, 2, -1, 0, 1)
                g_arrived(n, h, 2, 1)
            else:
                for d in (0, -1, 1, 2):
                    g_arrived(n, h, d, 2)

    def multiply(g):
        @pl.loop(0, 4)
        def _(n):
            lanes = pl.ds(pl.multiple_of(n * 256, 256), 256)
            acc[:, lanes] = jnp.dot(L[2 * g:2 * g + 2].reshape(256, 4096), R[:, lanes], preferred_element_type=F32)

    def contract(g):
        for q in range(16):
            for a in range(8):
                both = [acc[e * 128 + q * 8:e * 128 + q * 8 + 8, a * 128:(a + 1) * 128] for e in (0, 1)]
                lhs[a * 16:(a + 1) * 16, q * 128:(q + 1) * 128] = jnp.concatenate(both, axis=0).astype(BF16)

        @pl.loop(0, 4)
        def _(n):
            lanes = pl.ds(pl.multiple_of(n * 256, 256), 256)
            share = jnp.dot(lhs[...], W[:, lanes], preferred_element_type=F32)
            part[g, :, :, :, lanes] = share.reshape(8, 2, 8, 256)
        put(part.at[g, :, 1], sib.at[g], o_send.at[0, g], o_recv.at[0, g], (row_at(0, 1), col))

    def reduce(g):
        arrived(sib.at[g], o_send.at[0, g], o_recv.at[0, g])
        part[g, :, 0] = part[g, :, 0] + sib[g]
        if g > 0:
            put(part.at[g, :, 0], far.at[g - 1], o_send.at[1, g], o_recv.at[1, g], (row_at(GROUPS[g], 0), col))

    extra = {
        1: [lambda: r_stage1(0)], 3: [lambda: r_stage1(1)],
        5: [lambda: r_stage1(2)], 7: [lambda: r_stage1(3)],
        9: [lambda: r_stage2(0)], 10: [lambda: r_stage2(1)],
        11: [lambda: r_stage2(2)], 12: [lambda: r_stage2(3)],
        14: [r_stage3, lambda: multiply(0)],
        15: [lambda: contract(0)],
        17: [lambda: multiply(1), lambda: contract(1)],
        18: [lambda: reduce(0), lambda: reduce(1)],
        19: [lambda: multiply(2), lambda: contract(2)],
        20: [lambda: reduce(2)],
    }
    exchange_l(0, 1)
    exchange_l(1, 0)
    exchange_l(1, 1)
    r_stage0(0)
    for g in range(4):
        for e in (0, 1):
            if (g, e) != (0, 0):
                exchange_w(g, e)
    r_stage0(1)
    r_stage0(2)
    r_stage0(3)
    for g in (2, 3):
        for e in (0, 1):
            exchange_l(g, e)
    last = LAG * (len(ITEMS) - 1) + STAGES
    for tau in range(last):
        for n in range(len(ITEMS)):
            k = tau - LAG * n
            if 0 <= k < STAGES:
                stage(n, k)
        for do in extra.get(tau, ()):
            do()
    multiply(3)
    contract(3)
    reduce(3)
    for g in range(1, 4):
        arrived(far.at[g - 1], o_send.at[1, g], o_recv.at[1, g])
    out_ref[...] = part[0, :, 0] + far[0] + far[1] + far[2]
    for copy in sent:
        copy.wait_send()


def body(left_tiles, right_tiles, left_mask, right_mask, cycle_weight):
    vmem = pl.BlockSpec(memory_space=pltpu.VMEM)
    smem = pl.BlockSpec(memory_space=pltpu.SMEM)
    dma = pltpu.SemaphoreType.DMA
    total = pl.pallas_call(
        kernel,
        out_shape=jax.ShapeDtypeStruct((8, 8, 1024), F32),
        in_specs=[vmem, vmem, vmem, smem, smem],
        out_specs=vmem,
        scratch_shapes=[
            pltpu.VMEM((8, 128, 4096), BF16),
            pltpu.VMEM((4096, 1024), BF16),
            pltpu.VMEM((2048, 1024), BF16),
            pltpu.VMEM((2, 1024, 128), F32),
            pltpu.VMEM((8, 128, 256), BF16),
            pltpu.VMEM((256, 1024), F32),
            pltpu.VMEM((128, 2048), BF16),
            pltpu.VMEM((4, 8, 2, 8, 1024), F32),
            pltpu.VMEM((4, 8, 8, 1024), F32),
            pltpu.VMEM((3, 8, 8, 1024), F32),
            dma((len(ITEMS), 2, 15)),
            dma((len(ITEMS), 2, 16)),
            dma((2, 8)),
            dma((2, 8)),
            dma((28,)),
            dma((4, 4)),
            dma,
            dma((4, 4)),
            dma((2, 4)),
            dma((2, 4)),
        ],
        compiler_params=pltpu.CompilerParams(
            collective_id=0, has_side_effects=True, vmem_limit_bytes=56 * 1024 * 1024),
        cost_estimate=pl.CostEstimate(flops=11 * 10**9, bytes_accessed=4 * 2**20, transcendentals=0),
    )(left_tiles, right_tiles, cycle_weight, left_mask, right_mask)
    return jnp.swapaxes(total, 0, 1)


def solution(mesh):
    placed = (P("row", "col"), P("row", "col"), P("row", "col"), P("row", "col"), P("col", "row"))
    return jax.shard_map(
        body, mesh=mesh, in_specs=placed, out_specs=P("row", "col", None), check_vma=False
    )
```

time: 281 us -> 120 us (0.43)
  waiting for transfers between devices: 236 us -> 0 us
  Pallas kernels: 0 us -> 116 us
  matrix products: 19.1 us -> 0 us
  between operations: 13.2 us -> 0.01 us
  starting transfers between devices: 4.79 us -> 0 us
  other arithmetic: 3.97 us -> 0 us
    all_gather x3 -> x0, waiting for transfers between devices: 139 us -> none  [the longest x1 79.6 us: body(): gathered = lax.all_gather(masked_left, 'col', axis=1, tiled=True)]
    pallas_call x0 -> x1, Pallas kernels: none -> 116 us  [body(): pl.pallas_call(kernel, out_shape=jax.ShapeDtypeStruct((8, 8, 1024), F32),...]
    reduce_scatter x1 -> x0, waiting for transfers between devices: 78.7 us -> none  [body(): return lax.psum_scatter(cycle_terms, 'col', scatter_dimension=1, tiled=True)]
    dot_general x2 -> x0, matrix products: 19.1 us -> none  [the longest x1 13.7 us: body(): jnp.dot(gathered, lax.all_gather(masked_right, 'row', axis=0, tiled=True)...]
    all_to_all x1 -> x0, waiting for transfers between devices: 17.1 us -> none  [body(): lax.all_to_all(pair_block, 'col', split_axis=1, concat_axis=2, tiled=True)]
    all_to_all x1 -> x0, starting transfers between devices: 4.66 us -> none  [body(): lax.all_to_all(pair_block, 'col', split_axis=1, concat_axis=2, tiled=True)]
    mul x2 -> x0, other arithmetic: 3.28 us -> none  [apply_mask(): shaped * mask[:, None, :, None].astype(tiles.dtype)]
  transfers between devices with their start and end apart: 5 -> 0, of which waited for: 5 -> 0; matrix products, arithmetic and copies ran while one was open for 6% -> 0% of each run, Pallas kernels for 0% -> 0%
where the time goes in v1:
time: 120 us; the launch traced here: 119 us
  Pallas kernels  116 us (97%)
  local copies, waits for them, and re-layouts  3.15 us (3%)
    pallas_call x1, Pallas kernels, body(): pl.pallas_call(kernel, out_shape=jax.ShapeDtypeStruct((8, 8, 1024), F32),...  116 us

profile of v1, /device:TPU:1, one launch (start us, length us, event | category | flops | bytes accessed | tf_op | source)
XLA Modules:
  0.0 119.4 jit_solution(9729301421197226730)
XLA Ops:
  0.0 1.3 %copy.6.lm_ref = s32[8,2]{1,0:T(8,128)} copy(s32[8,2]{0,1:T(2,128)} %param.7) | data formatting | bytes 128 | tf_op args[2]
  1.3 116.3 %shard_map.55 = f32[8,8,1024]{2,1,0:T(8,128)} custom-call(bf16[1024,256]{1,0:T(8,128)(2,1)} %l_ref.1, bf16[512,1024]{1,0:T(8,128)(2,1)} %r_ref.1, bf16[1024,128]{1,0:T(8,128)(2,1)} %w_ref.1, s32[8,2]{1,0:T(8,128)} %copy.6.lm_ref, s32[4,8]{1,0:T(4,128)} %rm_ref.1), custom_call_target="tpu_custom_call" | custom-call | flops 11000000512 | bytes 4194304 | tf_op jit(solution)/shard_map/pallas_call | solution.py:277
  117.6 1.8 %copy.7 = f32[8,8,1024]{2,1,0:T(8,128)} copy(f32[8,8,1024]{2,0,1:T(8,128)} %bitcast.1) | data formatting | bytes 524288 | tf_op jit(solution)/shard_map/transpose | solution.py:308

commit v2 on v1

v2 whole, which is shorter than its diff:
```python
import jax
import jax.numpy as jnp
from jax import lax
from jax.experimental import pallas as pl
from jax.experimental.pallas import tpu as pltpu
from jax.sharding import PartitionSpec as P

MESH = pl.DeviceIdType.MESH
F32 = jnp.float32
BF16 = jnp.bfloat16

GROUPS = (0, 2, -1, 1)
ITEMS = (("S", 0), ("L", 1), ("W", 0), ("W", 1), ("L", 2), ("L", 3), ("S", 1))
GROUP_ITEMS = tuple(tuple(n for n, (kind, m) in enumerate(ITEMS) if (kind, m) in (("L", g), ("S", 2 * g), ("S", 2 * g + 1))) for g in range(4))
W_ITEMS = tuple(n for n, (kind, _) in enumerate(ITEMS) if kind == "W")


RATE = 42000.0
NEAR_RATE = 300000.0
LATENCY = 4.0
NEAR_LATENCY = 1.0
BACKLOG = 10.0
DEPTH = 7


NEAR = tuple((dy, dz) for dy in (-1, 0, 1) for dz in (-1, 0, 1))
FAR = tuple((dy, dz) for dy in (-1, 0, 1, 2) for dz in (-1, 0, 1, 2) if 2 in (dy, dz))


def norm(d):
    return (d + 1) % 4 - 1


def opposite(h, p, q):
    return ("y" if (p != 0) == (h == 0) else "z", p + q)


def tasks_of():
    tasks = {}
    for n, (kind, g) in enumerate(ITEMS):
        size = 32768 if kind == "S" else 65536
        for h in (0, 1):
            way = 1 if n % 2 == 0 else -1

            def go(p, q, ep, eq):
                return (("g", n, h, norm(p - ep), norm(q - eq)), opposite(h, ep, eq), size)

            if kind == "W":
                needs = [("w", m) for m in range(1, 8)]
            elif kind == "S":
                needs = [("l", g)] if g else []
            else:
                needs = [("l", 2 * g + h)]
            sends = [go(0, 0, e, 0) for e in (1, -1)] + [go(0, 0, 0, e) for e in (1, -1)]
            before = [("start", n, 0)] if h else [("start", n - 1, 1)] if n else []
            if n >= DEPTH:
                before = before + [("got", n - DEPTH, m, 2, 2) for m in (0, 1)]
            tasks["start", n, h] = (needs, [("prep",)] + before, 0.15, sends, 5)
            for p in range(-1, 3):
                for q in range(-1, 3):
                    if (p, q) == (0, 0):
                        continue
                    sends = []
                    if q == 0:
                        if p == -way:
                            sends.append(go(p, 0, way, 0))
                        sends += [go(p, 0, 0, e) for e in (1, -1)]
                    elif q == -1 and p in (0, 2):
                        sends.append(go(p, q, 0, 1))
                    elif q == 1 and p in (-1, 1):
                        sends.append(go(p, q, 0, -1))
                    tasks["got", n, h, p, q] = ([("g", n, h, p, q)], [("start", n, h)], 0.05 * (1 + len(sends)), sends, 10 + n)
    for p in range(4):
        sends = [(("r", -1, p), ("x", 1), 262144), (("r", 1, p), ("x", -1), 262144), (("s", 0, p), ("near", 0), 262144)]
        tasks["rstart", p] = ([], [("prep",)] + [("rstart", m) for m in range(p)], 0.5, sends, 40 + p)
        for d in (-1, 1):
            sends = [(("s", d, p), ("near", 0), 262144)]
            if (p < 2) == (d == -1):
                sends.append((("r", 2, p), ("x", -d), 262144))
            tasks["rgot", d, p] = ([("r", d, p)], [("rstart", p)], 0.1, sends, 20)
        tasks["rgot", 2, p] = ([("r", 2, p)], [("rstart", p)], 0.1, [(("s", 2, p), ("near", 0), 262144)], 20)
    tasks["rall",] = ([("s", d, p) for d in GROUPS for p in range(4)], [("rgot", d, p) for d in (-1, 1, 2) for p in range(4)], 0.1, [], 25)
    far = {-1: ("x", -1), 1: ("x", 1), 2: ("xx", 0)}
    for g in range(4):
        for e in (0, 1):
            slot = 2 * g + e
            if slot == 0:
                continue
            link = far.get(GROUPS[g], ("near", 0))
            tasks["lswap", g, e] = ([], [("prep",)], 0.05, [(("l", slot), link, 65536)], (30 if g in (0, 1) else 47))
            tasks["wswap", g, e] = ([], [("prep",)], 0.05, [(("w", slot), link, 32768)], 41)
    tasks["prep",] = ([], [], 2.0, [], 0)

    def arrived(items, halves=(0, 1)):
        return [(k, n, h, p, q) for n in items for h in halves for p in range(-1, 3) for q in range(-1, 3)
                for k in ("got",) if (p, q) != (0, 0)]

    def near(items):
        return [name for name in arrived(items) if 2 not in name[3:]]

    weights = arrived(W_ITEMS)
    for g in (1, 2, 3):
        for t in range(4):
            if g == 3:
                tasks["mul", g, t] = ([], [("rall",)] + near(GROUP_ITEMS[g]), 0.6, [], 60 + g)
                tasks["add", g, t] = ([], [("mul", g, t)] + arrived(GROUP_ITEMS[g]), 0.45, [], 60 + g)
            else:
                tasks["mul", g, t] = ([], [("rall",)] + arrived(GROUP_ITEMS[g]), 0.8, [], 60 + g)
        tasks["lhs", g] = ([], [("add" if g == 3 else "mul", g, t) for t in range(4)] + weights, 0.5, [], 60 + g)
        for u in (0, 1):
            tasks["con", g, u] = ([], [("lhs", g)] + [("con", g, 0)] * u, 0.6, [(("p", g, u), ("near", 0), 131072)], 55)
            tasks["red", g, u] = ([("p", g, u)], [("con", g, u)], 0.2, [(("f", g, u), far[GROUPS[g]], 65536)], 15)
            tasks["far", g, u] = ([("f", g, u)], [("red", g, u)], 0.1, [], 70)
    for e, n in enumerate(GROUP_ITEMS[0]):
        for t in range(4):
            tasks["blk", e, t] = ([], [("rall",)] + (near((n,)) if e else arrived((n,))), 0.4 if e else 0.6, [], 65)
            if e:
                tasks["bl2", e, t] = ([], [("blk", e, t)] + arrived((n,)), 0.35, [], 65)
    tasks["lhs", 0] = ([], [("bl2" if e else "blk", e, t) for e in (0, 1) for t in range(4)] + weights, 0.5, [], 66)
    for u in (0, 1):
        tasks["con", 0, u] = ([], [("lhs", 0)] + [("con", 0, 0)] * u, 0.6, [(("p", 0, u), ("near", 0), 131072)], 65)
        tasks["red", 0, u] = ([("p", 0, u)], [("con", 0, u)], 0.2, [], 70)
    return tasks


def schedule():
    tasks = tasks_of()
    free, arrival, done, order = {}, {}, set(), []
    now = 0.0
    while len(order) < len(tasks):
        ready, soonest = [], None
        for name, (needs, after, _, sends, rank) in tasks.items():
            if name in done or not all(a in done for a in after) or not all(m in arrival for m in needs):
                continue
            at = max([arrival[m] for m in needs], default=0.0)
            if name[0] == "start":
                at = max([at] + [sum(free.get(link, 0.0) for _, link, _ in sends) / len(sends) - BACKLOG])
            if at <= now:
                ready.append((rank, at, name))
            elif soonest is None or at < soonest:
                soonest = at
        if not ready:
            now = soonest
            continue
        name = min(ready, key=lambda r: r[:2])[2]
        needs, after, takes, sends, _ = tasks[name]
        now += takes
        for message, link, size in sends:
            links = [("x", 1), ("x", -1)] if link[0] == "xx" else [link]
            rate = NEAR_RATE if link[0] == "near" else RATE
            for way in links:
                free[way] = max(free.get(way, 0.0), now) + size / rate
            arrival[message] = max(free[way] for way in links) + (NEAR_LATENCY if link[0] == "near" else LATENCY)
        done.add(name)
        order.append(name)
    return order, now


ORDER = schedule()[0]


def kernel(l_ref, r_ref, w_ref, lm_ref, rm_ref, out_ref,
           L, R, W, lf, lp, acc, lhs, part, sib, away, far,
           g_send, g_recv, a_send, a_recv, r_send, r_recv, s_send, s_recv, o_send, o_recv):
    row, col = lax.axis_index("row"), lax.axis_index("col")
    x, core = row // 2, row % 2
    y, z = col // 4, col % 4
    sent = []

    def row_at(dx, e):
        other = core if e == 0 else 1 - core
        return ((x + dx + 4) % 4) * 2 + other

    def col_at(dy, dz):
        return ((y + dy + 4) % 4) * 4 + (z + dz + 4) % 4

    def put(src, dst, send, recv, device):
        copy = pltpu.make_async_remote_copy(
            src_ref=src, dst_ref=dst, send_sem=send, recv_sem=recv,
            device_id=device, device_id_type=MESH)
        copy.start()
        sent.append(copy)

    def arrived(dst, send, recv):
        pltpu.make_async_remote_copy(
            src_ref=dst, dst_ref=dst, send_sem=send, recv_sem=recv,
            device_id=(row_at(0, 1), col), device_id_type=MESH).wait_recv()

    barrier = pltpu.get_barrier_semaphore()
    peers = [(row, col_at(1, 0)), (row, col_at(-1, 0)), (row, col_at(0, 1)), (row, col_at(0, -1))]
    peers += [(row_at(dx, e), col) for dx in GROUPS for e in (0, 1) if (dx, e) != (0, 0)]
    for peer in peers:
        pl.semaphore_signal(barrier, inc=1, device_id=peer, device_id_type=MESH)

    for i in range(8):
        for t in range(2):
            keep = lm_ref[t, i].astype(F32)
            lf[t, i * 128:(i + 1) * 128, :] = l_ref[i * 128:(i + 1) * 128, t * 128:(t + 1) * 128].astype(F32) * keep
    for r in range(8):
        for t in range(2):
            for q in range(0, 16, 2):
                pair = [lf[t, pl.ds(8 * (q + s) + r, 8, stride=128), :] for s in (0, 1)]
                lp[r, q * 8:q * 8 + 16, t * 128:(t + 1) * 128] = jnp.concatenate(pair, axis=0).astype(BF16)
    own_l = pl.ds(pl.multiple_of(col * 256, 256), 256)
    own_w = pl.ds(pl.multiple_of(col * 128, 128), 128)
    row_w = pl.ds(pl.multiple_of(row * 128, 128), 128)
    L[0, :, own_l] = lp[row]

    pl.semaphore_wait(barrier, len(peers))

    def exchange_l(g, e):
        dx = GROUPS[g]
        slot = 2 * GROUPS.index(norm(-dx)) + e
        to = row_at(dx, e)
        put(lp.at[to], L.at[slot, :, own_l], a_send.at[0, 2 * g + e], a_recv.at[0, slot], (to, col))

    def exchange_w(g, e):
        dx = GROUPS[g]
        slot = 2 * GROUPS.index(norm(-dx)) + e
        to = row_at(dx, e)
        put(w_ref.at[pl.ds(pl.multiple_of(to * 128, 128), 128), :], W.at[own_w, row_w],
            a_send.at[1, 2 * g + e], a_recv.at[1, slot], (to, col))

    def exchanged_l(slot):
        arrived(L.at[slot, :, own_l], a_send.at[0, slot], a_recv.at[0, slot])

    def exchanged_w(slot):
        g, e = slot // 2, slot % 2
        lanes = pl.ds(pl.multiple_of(row_at(GROUPS[g], e) * 128, 128), 128)
        arrived(W.at[own_w, lanes], a_send.at[1, slot], a_recv.at[1, slot])

    def r_piece(dx, e, p):
        return R.at[pl.ds(pl.multiple_of(row_at(dx, e) * 512 + p * 128, 128), 128), :]

    r_count = [0]

    def r_put(dx, p, to):
        view = r_piece(dx, 0, p)
        if to is None:
            recv, device = s_recv.at[GROUPS.index(dx), p], (row_at(0, 1), col)
        else:
            recv, device = r_recv.at[GROUPS.index(norm(dx - to)), p], (row_at(to, 0), col)
        put(view, view, r_send.at[r_count[0]], recv, device)
        r_count[0] += 1

    def r_arrived(dx, p):
        arrived(r_piece(dx, 0, p), r_send.at[0], r_recv.at[GROUPS.index(dx), p])

    def r_start(p):
        here = pl.ds(pl.multiple_of(row * 512 + p * 128, 128), 128)
        for a in range(8):
            lanes = slice(a * 128, (a + 1) * 128)
            keep = rm_ref[p, a].astype(F32)
            R[here, lanes] = (r_ref[p * 128:(p + 1) * 128, lanes].astype(F32) * keep).astype(BF16)
        r_put(0, p, 1)
        r_put(0, p, -1)
        r_put(0, p, None)

    def r_got(d, p):
        r_arrived(d, p)
        if d != 2 and (p < 2) == (d == -1):
            r_put(d, p, -d)
        r_put(d, p, None)

    def r_all():
        for dx in GROUPS:
            for p in range(4):
                arrived(r_piece(dx, 1, p), s_send, s_recv.at[GROUPS.index(dx), p])

    def block(n, h, at):
        kind, g = ITEMS[n]
        lanes = pl.ds(pl.multiple_of(at * 256, 256), 256)
        if kind == "L":
            return L.at[2 * g + h, :, lanes]
        if kind == "S":
            return L.at[g, h * 64:(h + 1) * 64, lanes]
        return W.at[pl.ds(pl.multiple_of(at * 128 + (2 * g + h) * 32, 32), 32), :]

    def along(h, p, q):
        return col_at(p, q) if h == 0 else col_at(q, p)

    def sem_of(p, q):
        return 4 * (p % 4) + q % 4

    counts = {}

    def g_put(n, h, p, q, ep, eq):
        view = block(n, h, along(h, p, q))
        k = counts.get((n, h), 0)
        counts[n, h] = k + 1
        put(view, view, g_send.at[n, h, k], g_recv.at[n, h, sem_of(p - ep, q - eq)], (row, along(h, ep, eq)))

    def g_arrived(n, h, p, q):
        arrived(block(n, h, along(h, p, q)), g_send.at[n, h, 0], g_recv.at[n, h, sem_of(p, q)])

    def start(n, h):
        kind, g = ITEMS[n]
        if kind == "W" and (g, h) == (0, 0):
            W[own_w, row_w] = w_ref[row_w, :]
            for slot in range(1, 8):
                exchanged_w(slot)
        elif kind == "S" and g > 0 and h == 0:
            exchanged_l(g)
        elif kind == "L":
            exchanged_l(2 * g + h)
        for e in (1, -1):
            g_put(n, h, 0, 0, e, 0)
            g_put(n, h, 0, 0, 0, e)

    def got(n, h, p, q):
        g_arrived(n, h, p, q)
        way = 1 if n % 2 == 0 else -1
        if q == 0:
            if p == -way:
                g_put(n, h, p, 0, way, 0)
            for e in (1, -1):
                g_put(n, h, p, 0, 0, e)
        elif q == -1 and p in (0, 2):
            g_put(n, h, p, q, 0, 1)
        elif q == 1 and p in (-1, 1):
            g_put(n, h, p, q, 0, -1)

    def some(slots, lanes, offsets):
        total = None
        for dy, dz in offsets:
            at = pl.ds(pl.multiple_of(col_at(dy, dz) * 256, 256), 256)
            left = L[slots, :, at]
            term = jnp.dot(left.reshape(left.shape[0] * 128, 256), R[at, lanes], preferred_element_type=F32)
            total = term if total is None else total + term
        return total

    def multiply(g, t):
        lanes = slice(t * 256, (t + 1) * 256)
        if g == 3:
            acc[g, :, lanes] = some(slice(6, 8), lanes, NEAR)
        else:
            acc[g, :, lanes] = jnp.dot(L[2 * g:2 * g + 2].reshape(256, 4096), R[:, lanes], preferred_element_type=F32)

    def multiply_rest(g, t):
        lanes = slice(t * 256, (t + 1) * 256)
        acc[g, :, lanes] += some(slice(6, 8), lanes, FAR)

    def multiply_block(e, t):
        lanes = slice(t * 256, (t + 1) * 256)
        if e == 1:
            acc[0, 128:, lanes] = some(slice(1, 2), lanes, NEAR)
        else:
            acc[0, :128, lanes] = jnp.dot(L[0], R[:, lanes], preferred_element_type=F32)

    def multiply_block_rest(e, t):
        lanes = slice(t * 256, (t + 1) * 256)
        acc[0, 128:, lanes] += some(slice(1, 2), lanes, FAR)

    def left_of(g):
        for q in range(16):
            for a in range(8):
                both = [acc[g, e * 128 + q * 8:e * 128 + q * 8 + 8, a * 128:(a + 1) * 128] for e in (0, 1)]
                lhs[g, a * 16:(a + 1) * 16, q * 128:(q + 1) * 128] = jnp.concatenate(both, axis=0).astype(BF16)

    def contract(g, u):
        for t in (0, 1):
            lanes = slice(u * 512 + t * 256, u * 512 + (t + 1) * 256)
            share = jnp.dot(lhs[g], W[:, lanes], preferred_element_type=F32)
            part[g, u, :, :, :, t * 256:(t + 1) * 256] = share.reshape(8, 2, 8, 256)
        put(part.at[g, u, :, 1], sib.at[g, u], o_send.at[0, g, u], o_recv.at[0, g, u], (row_at(0, 1), col))

    def reduce(g, u):
        arrived(sib.at[g, u], o_send.at[0, g, u], o_recv.at[0, g, u])
        total = part[g, u, :, 0] + sib[g, u]
        if g == 0:
            part[g, u, :, 0] = total
        else:
            away[g - 1, u] = total.reshape(64, 512).astype(BF16)
            put(away.at[g - 1, u], far.at[g - 1, u], o_send.at[1, g, u], o_recv.at[1, g, u], (row_at(GROUPS[g], 0), col))

    def far_in(g, u):
        arrived(far.at[g - 1, u], o_send.at[1, g, u], o_recv.at[1, g, u])

    does = {
        "prep": lambda: None, "start": start, "got": got, "rstart": r_start, "rgot": r_got, "rall": r_all,
        "lswap": exchange_l, "wswap": exchange_w, "mul": multiply, "blk": multiply_block, "lhs": left_of, "con": contract,
        "add": multiply_rest, "bl2": multiply_block_rest, "red": reduce, "far": far_in,
    }
    for name, *which in ORDER:
        does[name](*which)
    for u in (0, 1):
        total = part[0, u, :, 0]
        for g in range(3):
            total = total + far[g, u].astype(F32).reshape(8, 8, 512)
        for a in range(8):
            out_ref[:, a, u * 512:(u + 1) * 512] = total[a]
    for copy in sent:
        copy.wait_send()


def body(left_tiles, right_tiles, left_mask, right_mask, cycle_weight):
    vmem = pl.BlockSpec(memory_space=pltpu.VMEM)
    smem = pl.BlockSpec(memory_space=pltpu.SMEM)
    dma = pltpu.SemaphoreType.DMA
    total = pl.pallas_call(
        kernel,
        out_shape=jax.ShapeDtypeStruct((8, 8, 1024), F32),
        in_specs=[vmem, vmem, vmem, smem, smem],
        out_specs=vmem,
        scratch_shapes=[
            pltpu.VMEM((8, 128, 4096), BF16),
            pltpu.VMEM((4096, 1024), BF16),
            pltpu.VMEM((2048, 1024), BF16),
            pltpu.VMEM((2, 1024, 128), F32),
            pltpu.VMEM((8, 128, 256), BF16),
            pltpu.VMEM((4, 256, 1024), F32),
            pltpu.VMEM((4, 128, 2048), BF16),
            pltpu.VMEM((4, 2, 8, 2, 8, 512), F32),
            pltpu.VMEM((4, 2, 8, 8, 512), F32),
            pltpu.VMEM((3, 2, 64, 512), BF16),
            pltpu.VMEM((3, 2, 64, 512), BF16),
            dma((len(ITEMS), 2, 15)),
            dma((len(ITEMS), 2, 16)),
            dma((2, 8)),
            dma((2, 8)),
            dma((28,)),
            dma((4, 4)),
            dma,
            dma((4, 4)),
            dma((2, 4, 2)),
            dma((2, 4, 2)),
        ],
        compiler_params=pltpu.CompilerParams(
            collective_id=0, has_side_effects=True, vmem_limit_bytes=56 * 1024 * 1024),
        cost_estimate=pl.CostEstimate(flops=11 * 10**9, bytes_accessed=4 * 2**20, transcendentals=0),
    )(left_tiles, right_tiles, cycle_weight, left_mask.T, right_mask)
    return total


def solution(mesh):
    placed = (P("row", "col"), P("row", "col"), P("row", "col"), P("row", "col"), P("col", "row"))
    return jax.shard_map(
        body, mesh=mesh, in_specs=placed, out_specs=P("row", "col", None), check_vma=False
    )
```

time: 120 us -> 103 us (0.86)
  Pallas kernels: 116 us -> 101 us
  local copies, waits for them, and re-layouts: 3.15 us -> 1.67 us
    pallas_call x1, Pallas kernels: 116 us -> 101 us  [body(): pl.pallas_call(kernel, out_shape=jax.ShapeDtypeStruct((8, 8, 1024), F32),...]
    transpose x1 -> x0, local copies, waits for them, and re-layouts: 1.81 us -> none  [body(): return jnp.swapaxes(total, 0, 1)]
where the time goes in v2:
time: 103 us; the launch traced here: 102 us
  Pallas kernels  101 us (98%)
  local copies, waits for them, and re-layouts  1.67 us (2%)
    pallas_call x1, Pallas kernels, body(): pl.pallas_call(kernel, out_shape=jax.ShapeDtypeStruct((8, 8, 1024), F32),...  101 us

profile of v2, /device:TPU:1, one launch (start us, length us, event | category | flops | bytes accessed | tf_op | source)
XLA Modules:
  0.0 102.5 jit_solution(8786521895383220940)
XLA Ops:
  0.0 100.8 %shard_map.55 = f32[8,8,1024]{2,1,0:T(8,128)} custom-call(bf16[1024,256]{1,0:T(8,128)(2,1)} %l_ref.1, bf16[512,1024]{1,0:T(8,128)(2,1)} %r_ref.1, bf16[1024,128]{1,0:T(8,128)(2,1)} %w_ref.1, s32[2,8]{1,0:T(2,128)} %bitcast.1, s32[4,8]{1,0:T(4,128)} %rm_ref.1), custom_call_target="tpu_custom_call" | custom-call | flops 11000000512 | bytes 4194304 | tf_op jit(solution)/shard_map/pallas_call | solution.py:400
  100.8 1.7 %copy.7 = f32[8,8,1024]{2,1,0:T(8,128)} copy(f32[8,8,1024]{2,1,0:T(8,128)} %shard_map.55) | data formatting | bytes 524288

commit v3 on v2

--- a/solution.py
+++ b/solution.py
@@ -10,25 +10,20 @@
 BF16 = jnp.bfloat16
 
 GROUPS = (0, 2, -1, 1)
-ITEMS = (("S", 0), ("L", 1), ("W", 0), ("W", 1), ("L", 2), ("L", 3), ("S", 1))
-GROUP_ITEMS = tuple(tuple(n for n, (kind, m) in enumerate(ITEMS) if (kind, m) in (("L", g), ("S", 2 * g), ("S", 2 * g + 1))) for g in range(4))
-W_ITEMS = tuple(n for n, (kind, _) in enumerate(ITEMS) if kind == "W")
-
-
+ITEMS = (("L", 0), ("L", 1), ("L", 2), ("L", 3), ("W", 0), ("W", 1))
 RATE = 42000.0
 NEAR_RATE = 300000.0
-LATENCY = 4.0
+LATENCY = 2.5
 NEAR_LATENCY = 1.0
-BACKLOG = 10.0
-DEPTH = 7
-
-
-NEAR = tuple((dy, dz) for dy in (-1, 0, 1) for dz in (-1, 0, 1))
-FAR = tuple((dy, dz) for dy in (-1, 0, 1, 2) for dz in (-1, 0, 1, 2) if 2 in (dy, dz))
+BACKLOG = 8.0
+DEPTH = 4
 
 
 def norm(d):
     return (d + 1) % 4 - 1
+
+
+LEAVES = tuple((p, 2) for p in (0, -1, 1, 2)) + ((0, 1), (2, 1), (-1, -1), (1, -1))
 
 
 def opposite(h, p, q):
@@ -38,7 +33,7 @@
 def tasks_of():
     tasks = {}
     for n, (kind, g) in enumerate(ITEMS):
-        size = 32768 if kind == "S" else 65536
+        size = 65536
         for h in (0, 1):
             way = 1 if n % 2 == 0 else -1
 
@@ -47,18 +42,16 @@
 
             if kind == "W":
                 needs = [("w", m) for m in range(1, 8)]
-            elif kind == "S":
-                needs = [("l", g)] if g else []
             else:
-                needs = [("l", 2 * g + h)]
+                needs = [("l", 2 * g + h)] if 2 * g + h else []
             sends = [go(0, 0, e, 0) for e in (1, -1)] + [go(0, 0, 0, e) for e in (1, -1)]
             before = [("start", n, 0)] if h else [("start", n - 1, 1)] if n else []
             if n >= DEPTH:
-                before = before + [("got", n - DEPTH, m, 2, 2) for m in (0, 1)]
+                needs = needs + [("g", n - DEPTH, m, 2, 2) for m in (0, 1)]
             tasks["start", n, h] = (needs, [("prep",)] + before, 0.15, sends, 5)
             for p in range(-1, 3):
                 for q in range(-1, 3):
-                    if (p, q) == (0, 0):
+                    if (p, q) == (0, 0) or (p, q) in LEAVES:
                         continue
                     sends = []
                     if q == 0:
@@ -87,39 +80,25 @@
             if slot == 0:
                 continue
             link = far.get(GROUPS[g], ("near", 0))
-            tasks["lswap", g, e] = ([], [("prep",)], 0.05, [(("l", slot), link, 65536)], (30 if g in (0, 1) else 47))
-            tasks["wswap", g, e] = ([], [("prep",)], 0.05, [(("w", slot), link, 32768)], 41)
+            tasks["lswap", g, e] = ([], [("prep",)], 0.05, [(("l", slot), link, 65536)], (30, 30, 40.5, 41.5)[g])
+            tasks["wswap", g, e] = ([], [("prep",)], 0.05, [(("w", slot), link, 32768)], 42.5)
     tasks["prep",] = ([], [], 2.0, [], 0)
 
     def arrived(items, halves=(0, 1)):
         return [(k, n, h, p, q) for n in items for h in halves for p in range(-1, 3) for q in range(-1, 3)
-                for k in ("got",) if (p, q) != (0, 0)]
-
-    def near(items):
-        return [name for name in arrived(items) if 2 not in name[3:]]
-
-    weights = arrived(W_ITEMS)
-    for g in (1, 2, 3):
+                for k in ("got",) if (p, q) != (0, 0) and (p, q) not in LEAVES]
+
+    def leaves(n, halves=(0, 1)):
+        return [("g", n, h, p, q) for h in halves for p, q in LEAVES]
+
+    for g in range(4):
         for t in range(4):
-            if g == 3:
-                tasks["mul", g, t] = ([], [("rall",)] + near(GROUP_ITEMS[g]), 0.6, [], 60 + g)
-                tasks["add", g, t] = ([], [("mul", g, t)] + arrived(GROUP_ITEMS[g]), 0.45, [], 60 + g)
-            else:
-                tasks["mul", g, t] = ([], [("rall",)] + arrived(GROUP_ITEMS[g]), 0.8, [], 60 + g)
-        tasks["lhs", g] = ([], [("add" if g == 3 else "mul", g, t) for t in range(4)] + weights, 0.5, [], 60 + g)
-        for u in (0, 1):
-            tasks["con", g, u] = ([], [("lhs", g)] + [("con", g, 0)] * u, 0.6, [(("p", g, u), ("near", 0), 131072)], 55)
-            tasks["red", g, u] = ([("p", g, u)], [("con", g, u)], 0.2, [(("f", g, u), far[GROUPS[g]], 65536)], 15)
-            tasks["far", g, u] = ([("f", g, u)], [("red", g, u)], 0.1, [], 70)
-    for e, n in enumerate(GROUP_ITEMS[0]):
-        for t in range(4):
-            tasks["blk", e, t] = ([], [("rall",)] + (near((n,)) if e else arrived((n,))), 0.4 if e else 0.6, [], 65)
-            if e:
-                tasks["bl2", e, t] = ([], [("blk", e, t)] + arrived((n,)), 0.35, [], 65)
-    tasks["lhs", 0] = ([], [("bl2" if e else "blk", e, t) for e in (0, 1) for t in range(4)] + weights, 0.5, [], 66)
-    for u in (0, 1):
-        tasks["con", 0, u] = ([], [("lhs", 0)] + [("con", 0, 0)] * u, 0.6, [(("p", 0, u), ("near", 0), 131072)], 65)
-        tasks["red", 0, u] = ([("p", 0, u)], [("con", 0, u)], 0.2, [], 70)
+            tasks["mul", g, t] = (leaves(g), [("rall",)] + arrived((g,)) + [("mul", g, 0)] * (t > 0), 0.85, [], 60 + g)
+    for u in range(4):
+        product = [("mul", g, t) for g in range(4) for t in range(4)]
+        tasks["con", u] = (leaves(4 + u // 2, (u % 2,)), product + arrived((4 + u // 2,), (u % 2,)), 0.8, [(("p", u), ("near", 0), 262144)], 55)
+        tasks["red", u] = ([("p", u)], [("con", u)], 0.3, [(("f", u, g), far[GROUPS[g]], 32768) for g in (1, 2, 3)], 15)
+        tasks["far", u] = ([("f", u, g) for g in (1, 2, 3)], [("red", u)], 0.3, [], 70)
     return tasks
 
 
@@ -160,7 +139,7 @@
 
 
 def kernel(l_ref, r_ref, w_ref, lm_ref, rm_ref, out_ref,
-           L, R, W, lf, lp, acc, lhs, part, sib, away, far,
+           L, R, W, lf, lp, lhs, part, sib, away, far,
            g_send, g_recv, a_send, a_recv, r_send, r_recv, s_send, s_recv, o_send, o_recv):
     row, col = lax.axis_index("row"), lax.axis_index("col")
     x, core = row // 2, row % 2
@@ -269,12 +248,10 @@
 
     def block(n, h, at):
         kind, g = ITEMS[n]
-        lanes = pl.ds(pl.multiple_of(at * 256, 256), 256)
         if kind == "L":
-            return L.at[2 * g + h, :, lanes]
-        if kind == "S":
-            return L.at[g, h * 64:(h + 1) * 64, lanes]
-        return W.at[pl.ds(pl.multiple_of(at * 128 + (2 * g + h) * 32, 32), 32), :]
+            return L.at[2 * g + h, :, pl.ds(pl.multiple_of(at * 256, 256), 256)]
+        u = 2 * g + h
+        return W.at[pl.ds(pl.multiple_of(at * 128, 128), 128), u * 256:(u + 1) * 256]
 
     def along(h, p, q):
         return col_at(p, q) if h == 0 else col_at(q, p)
@@ -299,9 +276,7 @@
             W[own_w, row_w] = w_ref[row_w, :]
             for slot in range(1, 8):
                 exchanged_w(slot)
-        elif kind == "S" and g > 0 and h == 0:
-            exchanged_l(g)
-        elif kind == "L":
+        elif kind == "L" and 2 * g + h > 0:
             exchanged_l(2 * g + h)
         for e in (1, -1):
             g_put(n, h, 0, 0, e, 0)
@@ -320,75 +295,45 @@
         elif q == 1 and p in (-1, 1):
             g_put(n, h, p, q, 0, -1)
 
-    def some(slots, lanes, offsets):
-        total = None
-        for dy, dz in offsets:
-            at = pl.ds(pl.multiple_of(col_at(dy, dz) * 256, 256), 256)
-            left = L[slots, :, at]
-            term = jnp.dot(left.reshape(left.shape[0] * 128, 256), R[at, lanes], preferred_element_type=F32)
-            total = term if total is None else total + term
-        return total
-
     def multiply(g, t):
-        lanes = slice(t * 256, (t + 1) * 256)
-        if g == 3:
-            acc[g, :, lanes] = some(slice(6, 8), lanes, NEAR)
-        else:
-            acc[g, :, lanes] = jnp.dot(L[2 * g:2 * g + 2].reshape(256, 4096), R[:, lanes], preferred_element_type=F32)
-
-    def multiply_rest(g, t):
-        lanes = slice(t * 256, (t + 1) * 256)
-        acc[g, :, lanes] += some(slice(6, 8), lanes, FAR)
-
-    def multiply_block(e, t):
-        lanes = slice(t * 256, (t + 1) * 256)
-        if e == 1:
-            acc[0, 128:, lanes] = some(slice(1, 2), lanes, NEAR)
-        else:
-            acc[0, :128, lanes] = jnp.dot(L[0], R[:, lanes], preferred_element_type=F32)
-
-    def multiply_block_rest(e, t):
-        lanes = slice(t * 256, (t + 1) * 256)
-        acc[0, 128:, lanes] += some(slice(1, 2), lanes, FAR)
-
-    def left_of(g):
+        if t == 0:
+            for h in (0, 1):
+                for p, q in LEAVES:
+                    g_arrived(g, h, p, q)
+        total = jnp.dot(L[2 * g:2 * g + 2].reshape(256, 4096), R[:, t * 256:(t + 1) * 256], preferred_element_type=F32)
         for q in range(16):
-            for a in range(8):
-                both = [acc[g, e * 128 + q * 8:e * 128 + q * 8 + 8, a * 128:(a + 1) * 128] for e in (0, 1)]
-                lhs[g, a * 16:(a + 1) * 16, q * 128:(q + 1) * 128] = jnp.concatenate(both, axis=0).astype(BF16)
-
-    def contract(g, u):
-        for t in (0, 1):
-            lanes = slice(u * 512 + t * 256, u * 512 + (t + 1) * 256)
-            share = jnp.dot(lhs[g], W[:, lanes], preferred_element_type=F32)
-            part[g, u, :, :, :, t * 256:(t + 1) * 256] = share.reshape(8, 2, 8, 256)
-        put(part.at[g, u, :, 1], sib.at[g, u], o_send.at[0, g, u], o_recv.at[0, g, u], (row_at(0, 1), col))
-
-    def reduce(g, u):
-        arrived(sib.at[g, u], o_send.at[0, g, u], o_recv.at[0, g, u])
-        total = part[g, u, :, 0] + sib[g, u]
-        if g == 0:
-            part[g, u, :, 0] = total
-        else:
-            away[g - 1, u] = total.reshape(64, 512).astype(BF16)
-            put(away.at[g - 1, u], far.at[g - 1, u], o_send.at[1, g, u], o_recv.at[1, g, u], (row_at(GROUPS[g], 0), col))
-
-    def far_in(g, u):
-        arrived(far.at[g - 1, u], o_send.at[1, g, u], o_recv.at[1, g, u])
+            for s in (0, 1):
+                both = [total[e * 128 + q * 8:e * 128 + q * 8 + 8, s * 128:(s + 1) * 128] for e in (0, 1)]
+                row0 = g * 128 + (2 * t + s) * 16
+                lhs[row0:row0 + 16, q * 128:(q + 1) * 128] = jnp.concatenate(both, axis=0).astype(BF16)
+
+    def contract(u):
+        for p, q in LEAVES:
+            g_arrived(4 + u // 2, u % 2, p, q)
+        share = jnp.dot(lhs[...], W[:, u * 256:(u + 1) * 256], preferred_element_type=F32)
+        part[u] = share.reshape(4, 8, 2, 8, 256)
+        put(part.at[u, :, :, 1], sib.at[u], o_send.at[u, 0], o_recv.at[u, 0], (row_at(0, 1), col))
+
+    def reduce(u):
+        arrived(sib.at[u], o_send.at[u, 0], o_recv.at[u, 0])
+        for g in (1, 2, 3):
+            away[g - 1, u] = (part[u, g, :, 0] + sib[u, g]).reshape(64, 256).astype(BF16)
+            put(away.at[g - 1, u], far.at[g - 1, u], o_send.at[u, g], o_recv.at[u, g], (row_at(GROUPS[g], 0), col))
+
+    def far_in(u):
+        total = part[u, 0, :, 0] + sib[u, 0]
+        for g in (1, 2, 3):
+            arrived(far.at[g - 1, u], o_send.at[u, g], o_recv.at[u, g])
+            total = total + far[g - 1, u].astype(F32).reshape(8, 8, 256)
+        for a in range(8):
+            out_ref[:, a, u * 256:(u + 1) * 256] = total[a]
 
     does = {
         "prep": lambda: None, "start": start, "got": got, "rstart": r_start, "rgot": r_got, "rall": r_all,
-        "lswap": exchange_l, "wswap": exchange_w, "mul": multiply, "blk": multiply_block, "lhs": left_of, "con": contract,
-        "add": multiply_rest, "bl2": multiply_block_rest, "red": reduce, "far": far_in,
+        "lswap": exchange_l, "wswap": exchange_w, "mul": multiply, "con": contract, "red": reduce, "far": far_in,
     }
     for name, *which in ORDER:
         does[name](*which)
-    for u in (0, 1):
-        total = part[0, u, :, 0]
-        for g in range(3):
-            total = total + far[g, u].astype(F32).reshape(8, 8, 512)
-        for a in range(8):
-            out_ref[:, a, u * 512:(u + 1) * 512] = total[a]
     for copy in sent:
         copy.wait_send()
 
@@ -408,12 +353,11 @@
             pltpu.VMEM((2048, 1024), BF16),
             pltpu.VMEM((2, 1024, 128), F32),
             pltpu.VMEM((8, 128, 256), BF16),
-            pltpu.VMEM((4, 256, 1024), F32),
-            pltpu.VMEM((4, 128, 2048), BF16),
-            pltpu.VMEM((4, 2, 8, 2, 8, 512), F32),
-            pltpu.VMEM((4, 2, 8, 8, 512), F32),
-            pltpu.VMEM((3, 2, 64, 512), BF16),
-            pltpu.VMEM((3, 2, 64, 512), BF16),
+            pltpu.VMEM((512, 2048), BF16),
+            pltpu.VMEM((4, 4, 8, 2, 8, 256), F32),
+            pltpu.VMEM((4, 4, 8, 8, 256), F32),
+            pltpu.VMEM((3, 4, 64, 256), BF16),
+            pltpu.VMEM((3, 4, 64, 256), BF16),
             dma((len(ITEMS), 2, 15)),
             dma((len(ITEMS), 2, 16)),
             dma((2, 8)),
@@ -422,8 +366,8 @@
             dma((4, 4)),
             dma,
             dma((4, 4)),
-            dma((2, 4, 2)),
-            dma((2, 4, 2)),
+            dma((4, 4)),
+            dma((4, 4)),
         ],
         compiler_params=pltpu.CompilerParams(
             collective_id=0, has_side_effects=True, vmem_limit_bytes=56 * 1024 * 1024),

time: 103 us -> 97.1 us (0.943)
  Pallas kernels: 101 us -> 95.3 us
    pallas_call x1, Pallas kernels: 101 us -> 95.3 us  [body(): pl.pallas_call(kernel, out_shape=jax.ShapeDtypeStruct((8, 8, 1024), F32),...]
where the time goes in v3:
time: 97.1 us; the launch traced here: 97 us
  Pallas kernels  95.3 us (98%)
  local copies, waits for them, and re-layouts  1.67 us (2%)
    pallas_call x1, Pallas kernels, body(): pl.pallas_call(kernel, out_shape=jax.ShapeDtypeStruct((8, 8, 1024), F32),...  95.3 us

profile of v3, /device:TPU:1, one launch (start us, length us, event | category | flops | bytes accessed | tf_op | source)
XLA Modules:
  0.0 97.0 jit_solution(209460117249286132)
XLA Ops:
  0.0 95.3 %shard_map.55 = f32[8,8,1024]{2,1,0:T(8,128)} custom-call(bf16[1024,256]{1,0:T(8,128)(2,1)} %l_ref.1, bf16[512,1024]{1,0:T(8,128)(2,1)} %r_ref.1, bf16[1024,128]{1,0:T(8,128)(2,1)} %w_ref.1, s32[2,8]{1,0:T(2,128)} %bitcast.1, s32[4,8]{1,0:T(4,128)} %rm_ref.1), custom_call_target="tpu_custom_call" | custom-call | flops 11000000512 | bytes 4194304 | tf_op jit(solution)/shard_map/pallas_call | solution.py:345
  95.3 1.7 %copy.7 = f32[8,8,1024]{2,1,0:T(8,128)} copy(f32[8,8,1024]{2,1,0:T(8,128)} %shard_map.55) | data formatting | bytes 524288

commit v4 on v3

--- a/solution.py
+++ b/solution.py
@@ -11,11 +11,11 @@
 
 GROUPS = (0, 2, -1, 1)
 ITEMS = (("L", 0), ("L", 1), ("L", 2), ("L", 3), ("W", 0), ("W", 1))
-RATE = 42000.0
+RATE = 43000.0
 NEAR_RATE = 300000.0
 LATENCY = 2.5
 NEAR_LATENCY = 1.0
-BACKLOG = 8.0
+BACKLOG = 6.0
 DEPTH = 4
 
 

time: 97.1 us -> 94 us (0.968)
  Pallas kernels: 95.3 us -> 91.7 us
    pallas_call x1, Pallas kernels: 95.3 us -> 91.7 us  [body(): pl.pallas_call(kernel, out_shape=jax.ShapeDtypeStruct((8, 8, 1024), F32),...]
where the time goes in v4:
time: 94 us; the launch traced here: 93.4 us
  Pallas kernels  91.7 us (98%)
  local copies, waits for them, and re-layouts  1.67 us (2%)
    pallas_call x1, Pallas kernels, body(): pl.pallas_call(kernel, out_shape=jax.ShapeDtypeStruct((8, 8, 1024), F32),...  91.7 us

profile of v4, /device:TPU:1, one launch (start us, length us, event | category | flops | bytes accessed | tf_op | source)
XLA Modules:
  0.0 93.4 jit_solution(9556497020438622584)
XLA Ops:
  0.0 91.7 %shard_map.55 = f32[8,8,1024]{2,1,0:T(8,128)} custom-call(bf16[1024,256]{1,0:T(8,128)(2,1)} %l_ref.1, bf16[512,1024]{1,0:T(8,128)(2,1)} %r_ref.1, bf16[1024,128]{1,0:T(8,128)(2,1)} %w_ref.1, s32[2,8]{1,0:T(2,128)} %bitcast.1, s32[4,8]{1,0:T(4,128)} %rm_ref.1), custom_call_target="tpu_custom_call" | custom-call | flops 11000000512 | bytes 4194304 | tf_op jit(solution)/shard_map/pallas_call | solution.py:345
  91.7 1.7 %copy.7 = f32[8,8,1024]{2,1,0:T(8,128)} copy(f32[8,8,1024]{2,1,0:T(8,128)} %shard_map.55) | data formatting | bytes 524288

commit v5 on v4

--- a/solution.py
+++ b/solution.py
@@ -15,7 +15,7 @@
 NEAR_RATE = 300000.0
 LATENCY = 2.5
 NEAR_LATENCY = 1.0
-BACKLOG = 6.0
+BACKLOG = 5.0
 DEPTH = 4
 
 

time: 94 us -> 98.3 us (1.046)
  Pallas kernels: 91.7 us -> 96.5 us
    pallas_call x1, Pallas kernels: 91.7 us -> 96.5 us  [body(): pl.pallas_call(kernel, out_shape=jax.ShapeDtypeStruct((8, 8, 1024), F32),...]
where the time goes in v5:
time: 98.3 us; the launch traced here: 98.1 us
  Pallas kernels  96.5 us (98%)
  local copies, waits for them, and re-layouts  1.67 us (2%)
    pallas_call x1, Pallas kernels, body(): pl.pallas_call(kernel, out_shape=jax.ShapeDtypeStruct((8, 8, 1024), F32),...  96.5 us

profile of v5, /device:TPU:1, one launch (start us, length us, event | category | flops | bytes accessed | tf_op | source)
XLA Modules:
  0.0 98.1 jit_solution(16441773651001734136)
XLA Ops:
  0.0 96.5 %shard_map.55 = f32[8,8,1024]{2,1,0:T(8,128)} custom-call(bf16[1024,256]{1,0:T(8,128)(2,1)} %l_ref.1, bf16[512,1024]{1,0:T(8,128)(2,1)} %r_ref.1, bf16[1024,128]{1,0:T(8,128)(2,1)} %w_ref.1, s32[2,8]{1,0:T(2,128)} %bitcast.1, s32[4,8]{1,0:T(4,128)} %rm_ref.1), custom_call_target="tpu_custom_call" | custom-call | flops 11000000512 | bytes 4194304 | tf_op jit(solution)/shard_map/pallas_call | solution.py:345
  96.5 1.7 %copy.7 = f32[8,8,1024]{2,1,0:T(8,128)} copy(f32[8,8,1024]{2,1,0:T(8,128)} %shard_map.55) | data formatting | bytes 524288
